TPU v7x, 512 devices: a whole 4x8x8 slice. The times are simulated.
512 devices in a mesh: seq: 16 (over z, y_hi), res: 32 (over y_lo, x, core).
Axes of the slice: x: 4, y: 8 (y_hi: 2, y_lo: 4; y = y_hi * 4 + y_lo), z: 8, core: 2. Of those that a mesh axis runs over, the one named last changes fastest.
Arguments:
- queries: bfloat16 [64, 2048, 384], P('seq', 'res'), may hold values from -64 to 64
- keys: bfloat16 [64, 2048, 384], P('seq', 'res'), may hold values from -4 to 4
- values: bfloat16 [64, 2048, 384], P('seq', 'res'), may hold values from -6 to 6
Outputs:
- attended: bfloat16 [64, 2048, 384], P('seq', 'res')
All inputs are finite; a program needn't handle non-finite values.
Results may differ from a plain program's by a relative error of at most 0.0049.
Values may be sent and summed in bfloat16 or wider, within the bound.
A program may use at most 64 MiB of HBM per device.

v0:
```python
import jax
import jax.numpy as jnp
from jax import lax
from jax.sharding import PartitionSpec as P

HEADS = 6


def local(queries, keys, values):
    row_dev, col_dev, width = queries.shape
    head_index = width // HEADS
    total_rows = row_dev * lax.axis_size("seq")
    scale = head_index ** (-0.5) / total_rows**0.5
    query_four = queries.reshape(row_dev, col_dev, HEADS, head_index)
    piece = lax.all_gather(keys, "res", axis=1, tiled=True)
    key_four = piece.reshape(row_dev, piece.shape[1], HEADS, head_index)
    partial_value = jnp.einsum(
        "rihe,rjhe->hij", query_four, key_four, preferred_element_type=jnp.float32
    )
    summed = lax.psum(partial_value, "seq") * scale
    probs = jax.nn.softmax(summed, axis=-1).astype(jnp.bfloat16)
    piece = lax.all_gather(values, "res", axis=1, tiled=True)
    count = piece.shape[1]
    value_four = piece.reshape(row_dev, count, HEADS, head_index)
    mixed = jnp.einsum("hij,rjhe->rihe", probs, value_four, preferred_element_type=jnp.float32)
    return mixed.astype(jnp.bfloat16).reshape(row_dev, col_dev, width)


def solution(mesh):
    return jax.shard_map(
        local,
        mesh=mesh,
        in_specs=(P("seq", "res", None), P("seq", "res", None), P("seq", "res", None)),
        out_specs=P("seq", "res", None),
        check_vma=False,
    )
```

profile of v0, /device:TPU:1, one launch (start us, length us, event | category | flops | bytes accessed | tf_op | source)
XLA Modules:
  0.0 479.1 jit_solution(10596451625591247274)
XLA Ops:
  6.5 0.0 all-gather.3.cloned.1.call-start
  6.5 1.8 copy.11
  8.3 0.0 all-gather.3.cloned.1.call-update
  8.3 0.0 all-gather.5.cloned.1.call-start
  8.4 1.8 copy.15
  10.1 0.0 all-gather.5.cloned.1.call-update
  10.2 0.0 all-reduce.2.cloned.1.call-start
  10.2 1.2 reshape.14
  11.5 72.8 %all-gather.3.cloned.1.call-done = bf16[4,2048,384]{2,0,1:T(4,128)(2,1)} async-done(((bf16[4,64,384]{2,0,1:T(4,128)(2,1)}), bf16[4,2048,384]{2,0,1:T(4,128)(2,1)}) %all-gather.3.cloned.1.call-update) | async-done | bytes 6291472 | tf_op jit(solution)/shard_map/all_gather | solution.py:15
  84.3 10.6 %copy.12 = bf16[4,2048,384]{1,2,0:T(8,128)(2,1)} copy(bf16[4,2048,384]{2,0,1:T(4,128)(2,1)} %all-gather.3.cloned.1.call-done) | data formatting | bytes 12582912 | tf_op jit(solution)/shard_map/all_gather | solution.py:15
  94.9 5.7 %fusion.7 = f32[6,64,2048]{2,1,0:T(8,128)} fusion(bf16[4,2048,6,64]{1,3,2,0:T(8,128)(2,1)} %bitcast.16, bf16[4,64,6,64]{3,2,1,0:T(8,128)(2,1)S(1)} %reshape.14), kind=kOutput, calls=%fused_computation.8 | convolution fusion | flops 402653184 | bytes 9633792 | tf_op jit(solution)/shard_map/rihe,rjhe->hij/dot_general | solution.py:17
  100.6 0.0 all-reduce.2.cloned.1.call-update
  100.7 54.3 %all-gather.5.cloned.1.call-done = bf16[4,2048,384]{2,0,1:T(4,128)(2,1)} async-done(((bf16[4,64,384]{2,0,1:T(4,128)(2,1)}), bf16[4,2048,384]{2,0,1:T(4,128)(2,1)}) %all-gather.5.cloned.1.call-update) | async-done | bytes 6291472 | tf_op jit(solution)/shard_map/all_gather | solution.py:22
  154.9 10.6 %copy.16 = bf16[4,2048,384]{1,2,0:T(8,128)(2,1)} copy(bf16[4,2048,384]{2,0,1:T(4,128)(2,1)} %all-gather.5.cloned.1.call-done) | data formatting | bytes 12582912 | tf_op jit(solution)/shard_map/all_gather | solution.py:22
  165.6 296.0 %all-reduce.2.cloned.1.call-done = f32[6,64,2048]{2,1,0:T(8,128)} async-done(((f32[6,64,2048]{2,1,0:T(8,128)}), f32[6,64,2048]{2,1,0:T(8,128)}) %all-reduce.2.cloned.1.call-update) | async-done | bytes 3145744 | tf_op jit(solution)/shard_map/psum | solution.py:20
  461.6 2.7 fusion.32
  464.3 6.9 %fusion.18 = bf16[4,64,6,64]{3,1,0,2:T(8,128)(2,1)S(1)} fusion(bf16[4,2048,6,64]{1,3,2,0:T(8,128)(2,1)} %bitcast.17, f32[6,64]{1,0:T(8,128)S(1)} %fusion.32, f32[6,64,2048]{2,1,0:T(8,128)} %all-reduce.2.cloned.1.call-done), kind=kOutput, calls=%fused_computation.14 | convolution fusion | flops 405899648 | bytes 9635328 | tf_op jit(solution)/shard_map/hij,rjhe->rihe/dot_general | solution.py:25
  471.3 0.3 copy.18
  471.6 1.0 reshape.17
Async XLA Ops:
  6.5 77.8 %all-gather.3.cloned.1.call-start = ((), (), s32[]{:S(2)}) async-start(), calls=%async_computation | async-start | bytes 6488064 | tf_op jit(solution)/shard_map/all_gather | solution.py:15
  8.3 146.6 %all-gather.5.cloned.1.call-start = ((), (), s32[]{:S(2)}) async-start(), calls=%async_computation.2 | async-start | bytes 6488064 | tf_op jit(solution)/shard_map/all_gather | solution.py:22
  10.2 451.4 %all-reduce.2.cloned.1.call-start = ((), (), s32[]{:S(2)}) async-start(), calls=%async_computation.1 | async-start | bytes 6291456 | tf_op jit(solution)/shard_map/psum | solution.py:20
Sparse Core Ops, SparseCore 0:
  9.5 74.7 all-gather.2
  86.4 68.4 all-gather.4
  157.9 303.6 all-reduce.1
where the time goes:
time: 481 us; the launch traced here: 479 us
  waiting for transfers between devices  423 us (88%)
  local copies, waits for them, and re-layouts  27.3 us (6%)
  between operations  13.1 us (3%)
  matrix products  12.7 us (3%)
    psum x1, waiting for transfers between devices, local(): summed = lax.psum(partial_value, 'seq') * scale  296 us
    all_gather x1, waiting for transfers between devices, local(): piece = lax.all_gather(keys, 'res', axis=1, tiled=True)  72.8 us
    all_gather x1, waiting for transfers between devices, local(): piece = lax.all_gather(values, 'res', axis=1, tiled=True)  54.3 us
    all_gather x1, local copies, waits for them, and re-layouts, local(): piece = lax.all_gather(values, 'res', axis=1, tiled=True)  10.6 us
    all_gather x1, local copies, waits for them, and re-layouts, local(): piece = lax.all_gather(keys, 'res', axis=1, tiled=True)  10.6 us
  transfers between devices with their start and end apart: 3, of which 3 were waited for; matrix products, arithmetic and copies ran while one was open for 6% of the time, Pallas kernels for 0%

commit v1 on v0

v1 whole, which is shorter than its diff:
```python
import functools

import jax
import jax.numpy as jnp
from jax import lax
from jax.experimental import pallas as pl
from jax.experimental.pallas import tpu as pltpu
from jax.sharding import PartitionSpec as P

NZ, NY, NX = 8, 8, 4
PAIRS = 3
ROWS, TOK, LANES = 4, 64, 128
F32, BF16 = jnp.float32, jnp.bfloat16


def kernel(
    q_hbm, k_hbm, v_hbm, out_hbm,
    kbuf, vbuf, qbuf, qsend, qm, kcat, sbuf, zrecv, stat, statv, pbuf, obuf, orecv, xrecv, oown, oswap,
    load_sem, out_sem, k_ss, k_rs, v_ss, v_rs, qs_ss, qs_rs, qx_ss, qx_rs, z_ss, z_rs, st_ss, st_rs,
    p_ss, p_rs, o_ss, o_rs, x_ss, x_rs, w_ss, w_rs,
):
    s_id, r_id = lax.axis_index("seq"), lax.axis_index("res")
    z, yh = s_id // 2, s_id % 2
    yl, x, c = r_id // 8, (r_id // 2) % 4, r_id % 2
    y = yh * 4 + yl

    def at(z_=None, y_=None, x_=None, c_=None):
        z_ = z if z_ is None else z_
        y_ = y if y_ is None else y_
        x_ = x if x_ is None else x_
        c_ = c if c_ is None else c_
        return {"seq": z_ * 2 + y_ // 4, "res": ((y_ % 4) * 4 + x_) * 2 + c_}

    def zdev(k):
        return at(z_=(z + k + NZ) % NZ)

    def ydev(k):
        return at(y_=(y + k + NY) % NY)

    partner = at(y_=(y + 4) % NY, c_=1 - c)
    sibling = at(c_=1 - c)

    def group(k):
        g = (x * 2 + c + k) % 8
        return at(x_=g // 2, c_=g % 2)

    def group_index(k):
        g = (x * 2 + c + k + 8) % 8
        return g // 2, g % 2

    def remote(src, dst, ss, rs, dev):
        return pltpu.make_async_remote_copy(
            src_ref=src, dst_ref=dst, send_sem=ss, recv_sem=rs, device_id=dev, device_id_type=pl.DeviceIdType.MESH
        )

    home = c == yh

    def lanes(p):
        return pl.ds(p * LANES, LANES)

    def load_k(p):
        return pltpu.make_async_copy(k_hbm.at[:, :, lanes(p)], kbuf.at[p, y], load_sem.at[0, p])

    def load_v(p):
        return pltpu.make_async_copy(v_hbm.at[:, :, lanes(p)], vbuf.at[p, y], load_sem.at[1, p])

    def load_q_home(p):
        return pltpu.make_async_copy(q_hbm.at[:, :, lanes(p)], qbuf.at[p, c, x], load_sem.at[2, p])

    def load_q_away(p):
        return pltpu.make_async_copy(q_hbm.at[:, :, lanes(p)], qsend.at[p], load_sem.at[2, p])

    def ring(buf, ss, rs, p, step, way):
        src = (y - way * (step - 1) + NY) % NY
        half = pl.ds(0, ROWS) if step < 4 else (pl.ds(0, 2) if way == 1 else pl.ds(2, 2))
        d = 0 if way == 1 else 1
        view = buf.at[p, src, half]
        return remote(view, view, ss.at[p, step - 1, d], rs.at[p, step - 1, d], ydev(way))

    def ring_recv(buf, ss, rs, p, step, way):
        src = (y - way * step + NY) % NY
        half = pl.ds(0, ROWS) if step < 4 else (pl.ds(0, 2) if way == 1 else pl.ds(2, 2))
        d = 0 if way == 1 else 1
        view = buf.at[p, src, half]
        return remote(view, view, ss.at[p, step - 1, d], rs.at[p, step - 1, d], ydev(way))

    def ring_start(buf, ss, rs, p, step):
        for way in (1, -1):
            ring(buf, ss, rs, p, step, way).start()

    def ring_wait(buf, ss, rs, p, step):
        for way in (1, -1):
            ring_recv(buf, ss, rs, p, step, way).wait_recv()

    def ring_end(buf, ss, rs, p):
        for step in range(1, 5):
            for way in (1, -1):
                ring(buf, ss, rs, p, step, way).wait_send()

    K = (kbuf, k_ss, k_rs)
    V = (vbuf, v_ss, v_rs)

    def q_swap(p):
        return remote(qsend.at[p], qbuf.at[p, 1 - c, x], qs_ss.at[p], qs_rs.at[p], partner)

    def q_swap_recv(p):
        return remote(qsend.at[p], qbuf.at[p, c, x], qs_ss.at[p], qs_rs.at[p], partner)

    def q_ready(p):
        @pl.when(home)
        def _():
            load_q_home(p).wait()

        @pl.when(jnp.logical_not(home))
        def _():
            q_swap_recv(p).wait_recv()

    def q_spread(p, k):
        view = qbuf.at[p, c, x]
        return remote(view, view, qx_ss.at[p, k - 1], qx_rs.at[p, k - 1], group(k))

    def q_spread_recv(p, k):
        gx, gc = group_index(-k)
        view = qbuf.at[p, gc, gx]
        return remote(view, view, qx_ss.at[p, k - 1], qx_rs.at[p, k - 1], group(k))

    lane = lax.broadcasted_iota(jnp.int32, (256, LANES), 1)

    def scores(p):
        for g in range(2):
            for r in range(ROWS):
                cols = pl.ds((g * ROWS + r) * LANES, LANES)
                block = qbuf[p, g, :, r].reshape(256, LANES)
                zero = jnp.zeros_like(block)
                qm[0:256, cols] = jnp.where(lane < 64, block, zero)
                qm[256:512, cols] = jnp.where(lane >= 64, block, zero)
                kcat[:, cols] = kbuf[p, g * 4 : g * 4 + 4, r].reshape(256, LANES)
        for half in range(2):
            part = lax.dot_general(
                qm[half * 256 : half * 256 + 256, :], kcat[...], (((1,), (1,)), ((), ())), preferred_element_type=F32
            )
            sbuf[p, half * 4 : half * 4 + 4] = part.reshape(4, TOK, 256)

    def zslice(way, step):
        return (z + way * (5 - step) + NZ) % NZ

    def z_copy(p, step, way):
        d = 0 if way == 1 else 1
        half = pl.ds(0, TOK) if step > 1 else pl.ds(d * 32, 32)
        return remote(
            sbuf.at[p, zslice(way, step), half],
            zrecv.at[p, d, step - 1, half],
            z_ss.at[p, step - 1, d],
            z_rs.at[p, step - 1, d],
            zdev(way),
        )

    def z_start(p, step):
        for way in (1, -1):
            z_copy(p, step, way).start()

    def z_add(p, step):
        for way in (1, -1):
            d = 0 if way == 1 else 1
            z_copy(p, step, way).wait_recv()
            s = zslice(way, step + 1)
            if step == 1:
                rows = pl.ds(d * 32, 32)
                sbuf[p, s, rows] = sbuf[p, s, rows] + zrecv[p, d, 0, rows]
            else:
                sbuf[p, s] = sbuf[p, s] + zrecv[p, d, step - 1]

    def stat_copy(p, k):
        return remote(stat.at[p, 0], stat.at[p, k], st_ss.at[p, k - 1], st_rs.at[p, k - 1], group(k))

    def softmax_local(p):
        for way in (1, -1):
            z_copy(p, 4, way).wait_recv()
        s = sbuf[p, z] + zrecv[p, 0, 3] + zrecv[p, 1, 3]
        s = s * (1.0 / 64.0)
        m = jnp.max(s, axis=1, keepdims=True)
        e = jnp.exp(s - m)
        l = jnp.sum(e, axis=1, keepdims=True)
        statv[p] = e
        col = lax.broadcasted_iota(jnp.int32, (TOK, LANES), 1)
        both = jnp.where(col == 0, m, l)
        tall = jnp.concatenate([both, both], axis=0)
        stat[p, 0] = jnp.transpose(tall)[0:8, :]
        for k in range(1, 8):
            stat_copy(p, k).start()

    def softmax_global(p):
        for k in range(1, 8):
            stat_copy(p, k).wait_recv()
        m = stat[p, 0, 0:1, :]
        for k in range(1, 8):
            m = jnp.maximum(m, stat[p, k, 0:1, :])
        l = jnp.zeros_like(m)
        for k in range(8):
            l = l + jnp.exp(stat[p, k, 0:1, :] - m) * stat[p, k, 1:2, :]
        factor = jnp.exp(stat[p, 0, 0:1, :] - m) / l
        tall = jnp.transpose(jnp.broadcast_to(factor, (LANES, LANES)))
        pbuf[p, z] = (statv[p] * tall[0:TOK, 0:1]).astype(BF16)
        for k in range(1, 8):
            p_copy(p, k).start()

    def p_copy(p, k):
        return remote(pbuf.at[p, z], pbuf.at[p, z], p_ss.at[p, k - 1], p_rs.at[p, k - 1], zdev(k))

    def p_recv(p, k):
        view = pbuf.at[p, (z - k + NZ) % NZ]
        return remote(view, view, p_ss.at[p, k - 1], p_rs.at[p, k - 1], zdev(k))

    def attend(p, g):
        probs = pbuf[p].reshape(512, 256)
        for r in range(0, ROWS, 2):
            vals = jnp.concatenate([vbuf[p, pl.ds(g * 4, 4), r + i].reshape(256, LANES) for i in range(2)], axis=1)
            o = lax.dot_general(probs, vals, (((1,), (0,)), ((), ())), preferred_element_type=F32)
            for i in range(2):
                cols = slice(i * LANES, (i + 1) * LANES)
                both = jnp.where(lane < 64, o[0:256, cols], o[256:512, cols])
                obuf[p, g, :, r + i] = both.reshape(NX, TOK, LANES)

    def o_copy(p):
        return remote(obuf.at[p, 1 - c], orecv.at[p], o_ss.at[p], o_rs.at[p], sibling)

    def x_copy(p, k):
        to = (x + k) % NX
        return remote(obuf.at[p, c, to], xrecv.at[p, k - 1], x_ss.at[p, k - 1], x_rs.at[p, k - 1], at(x_=to))

    def attend_all(p):
        for k in range(1, 8):
            p_recv(p, k).wait_recv()
        attend(p, 1 - c)
        o_copy(p).start()
        attend(p, c)

    def chip_sum(p):
        o_copy(p).wait_recv()
        for k in (2, 1, 3):
            to = (x + k) % NX
            obuf[p, c, to] = obuf[p, c, to] + orecv[p, to]
            x_copy(p, k).start()

    def out_home(p):
        return pltpu.make_async_copy(oown.at[p], out_hbm.at[:, :, lanes(p)], out_sem.at[p])

    def out_away(p):
        return pltpu.make_async_copy(oswap.at[p], out_hbm.at[:, :, lanes(p)], out_sem.at[p])

    def w_copy(p):
        return remote(oown.at[p], oswap.at[p], w_ss.at[p], w_rs.at[p], partner)

    def finish(p):
        total = obuf[p, c, x] + orecv[p, x]
        for k in (1, 2, 3):
            x_copy(p, k).wait_recv()
        total = total + xrecv[p, 0] + xrecv[p, 1] + xrecv[p, 2]
        oown[p] = total.astype(BF16)

        @pl.when(home)
        def _():
            out_home(p).start()

        @pl.when(jnp.logical_not(home))
        def _():
            w_copy(p).start()

    for p in range(PAIRS):
        load_k(p).start()

        @pl.when(home)
        def _():
            load_q_home(p).start()

        @pl.when(jnp.logical_not(home))
        def _():
            load_q_away(p).start()

    for p in range(PAIRS):
        load_v(p).start()

    barrier = pltpu.get_barrier_semaphore()
    peers = [zdev(k) for k in range(1, 8)] + [ydev(1), ydev(-1), partner] + [group(k) for k in range(1, 8)]
    for dev in peers:
        pl.semaphore_signal(barrier, inc=1, device_id=dev, device_id_type=pl.DeviceIdType.MESH)
    pl.semaphore_wait(barrier, len(peers))

    for p in range(PAIRS):
        load_k(p).wait()
        ring_start(*K, p, 1)

        @pl.when(jnp.logical_not(home))
        def _():
            load_q_away(p).wait()
            q_swap(p).start()

    for p in range(PAIRS):
        ring_wait(*K, p, 1)
        ring_start(*K, p, 2)
    for p in range(PAIRS):
        q_ready(p)
        for k in range(1, 8):
            q_spread(p, k).start()
    for p in range(PAIRS):
        ring_wait(*K, p, 2)
        ring_start(*K, p, 3)
    for p in range(PAIRS):
        ring_wait(*K, p, 3)
        ring_start(*K, p, 4)
    for p in range(PAIRS):
        load_v(p).wait()
        ring_start(*V, p, 1)
    for p in range(PAIRS):
        ring_wait(*K, p, 4)
        for k in range(1, 8):
            q_spread_recv(p, k).wait_recv()
        scores(p)
        z_start(p, 1)
    for step in (1, 2, 3):
        for p in range(PAIRS):
            z_add(p, step)
            z_start(p, step + 1)
        for p in range(PAIRS):
            ring_wait(*V, p, step)
            ring_start(*V, p, step + 1)
    for p in range(PAIRS):
        softmax_local(p)
    for p in range(PAIRS):
        softmax_global(p)
    for p in range(PAIRS):
        ring_wait(*V, p, 4)
    for p in range(PAIRS):
        attend_all(p)
        chip_sum(p)
    for p in range(PAIRS):
        finish(p)

    for p in range(PAIRS):
        @pl.when(home)
        def _():
            out_home(p).wait()

        @pl.when(jnp.logical_not(home))
        def _():
            w_copy(p).wait_recv()
            out_away(p).start()
            q_swap(p).wait_send()
            w_copy(p).wait_send()
            out_away(p).wait()

        ring_end(*K, p)
        ring_end(*V, p)
        for k in range(1, 8):
            q_spread(p, k).wait_send()
            stat_copy(p, k).wait_send()
            p_copy(p, k).wait_send()
        for step in range(1, 5):
            for way in (1, -1):
                z_copy(p, step, way).wait_send()
        o_copy(p).wait_send()
        for k in (1, 2, 3):
            x_copy(p, k).wait_send()


def local(queries, keys, values):
    vmem = pltpu.VMEM
    dma = pltpu.SemaphoreType.DMA
    block = (ROWS, TOK, LANES)
    return pl.pallas_call(
        kernel,
        out_shape=jax.ShapeDtypeStruct(queries.shape, BF16),
        in_specs=[pl.BlockSpec(memory_space=pl.ANY)] * 3,
        out_specs=pl.BlockSpec(memory_space=pl.ANY),
        scratch_shapes=[
            vmem((PAIRS, NY) + block, BF16),
            vmem((PAIRS, NY) + block, BF16),
            vmem((PAIRS, 2, NX) + block, BF16),
            vmem((PAIRS,) + block, BF16),
            vmem((512, 1024), BF16),
            vmem((256, 1024), BF16),
            vmem((PAIRS, NZ, TOK, 256), F32),
            vmem((PAIRS, 2, 4, TOK, 256), F32),
            vmem((PAIRS, 8, 8, LANES), F32),
            vmem((PAIRS, TOK, 256), F32),
            vmem((PAIRS, NZ, TOK, 256), BF16),
            vmem((PAIRS, 2, NX) + block, F32),
            vmem((PAIRS, NX) + block, F32),
            vmem((PAIRS, 3) + block, F32),
            vmem((PAIRS,) + block, BF16),
            vmem((PAIRS,) + block, BF16),
            dma((3, PAIRS)),
            dma((PAIRS,)),
            dma((PAIRS, 4, 2)), dma((PAIRS, 4, 2)),
            dma((PAIRS, 4, 2)), dma((PAIRS, 4, 2)),
            dma((PAIRS,)), dma((PAIRS,)),
            dma((PAIRS, 7)), dma((PAIRS, 7)),
            dma((PAIRS, 4, 2)), dma((PAIRS, 4, 2)),
            dma((PAIRS, 7)), dma((PAIRS, 7)),
            dma((PAIRS, 7)), dma((PAIRS, 7)),
            dma((PAIRS,)), dma((PAIRS,)),
            dma((PAIRS, 3)), dma((PAIRS, 3)),
            dma((PAIRS,)), dma((PAIRS,)),
        ],
        compiler_params=pltpu.CompilerParams(collective_id=0, has_side_effects=True, vmem_limit_bytes=40 << 20),
    )(queries, keys, values)


def solution(mesh):
    spec = P("seq", "res", None)
    return jax.shard_map(local, mesh=mesh, in_specs=(spec, spec, spec), out_specs=spec, check_vma=False)
```

time: 481 us -> 104 us (0.22)
  waiting for transfers between devices: 423 us -> 0 us
  Pallas kernels: 0 us -> 100 us
  local copies, waits for them, and re-layouts: 27.3 us -> 3.46 us
  between operations: 13.1 us -> 0.01 us
  matrix products: 12.7 us -> 0 us
    psum x1 -> x0, waiting for transfers between devices: 296 us -> none  [local(): summed = lax.psum(partial_value, 'seq') * scale]
    all_gather x2 -> x0, waiting for transfers between devices: 127 us -> none  [the longest x1 72.8 us: local(): piece = lax.all_gather(keys, 'res', axis=1, tiled=True)]
    pallas_call x0 -> x1, Pallas kernels: none -> 100 us  [local(): pl.pallas_call(kernel, out_shape=jax.ShapeDtypeStruct(queries.shape, BF16...]
    all_gather x2 -> x0, local copies, waits for them, and re-layouts: 21.2 us -> none  [the longest x1 10.6 us: local(): piece = lax.all_gather(values, 'res', axis=1, tiled=True)]
    dot_general x2 -> x0, matrix products: 12.7 us -> none  [the longest x1 6.95 us: local(): jnp.einsum('hij,rjhe->rihe', probs, value_four, preferred_element_type=jn...]
  transfers between devices with their start and end apart: 3 -> 0, of which waited for: 3 -> 0; matrix products, arithmetic and copies ran while one was open for 6% -> 0% of each run, Pallas kernels for 0% -> 0%
where the time goes in v1:
time: 104 us; the launch traced here: 103 us
  Pallas kernels  100 us (96%)
  local copies, waits for them, and re-layouts  3.46 us (3%)
    pallas_call x1, Pallas kernels, local(): pl.pallas_call(kernel, out_shape=jax.ShapeDtypeStruct(queries.shape, BF16...  100 us
    unnamed x7, local copies, waits for them, and re-layouts  3.46 us

profile of v1, /device:TPU:1, one launch (start us, length us, event | category | flops | bytes accessed | tf_op | source)
XLA Modules:
  0.0 103.5 jit_solution(360820136770808616)
XLA Ops:
  0.0 0.0 copy-start
  0.0 0.9 copy-done
  0.9 0.0 copy-start.1
  0.9 0.9 copy-done.1
  1.9 0.0 copy-start.2
  1.9 0.9 copy-done.2
  2.8 100.0 %shard_map.37 = bf16[4,64,384]{2,1,0:T(8,128)(2,1)S(1)} custom-call(bf16[4,64,384]{2,1,0:T(8,128)(2,1)S(1)} %copy-done, bf16[4,64,384]{2,1,0:T(8,128)(2,1)S(1)} %copy-done.1, bf16[4,64,384]{2,1,0:T(8,128)(2,1)S(1)} %copy-done.2), custom_call_target="tpu_custom_call" | custom-call | tf_op jit(solution)/shard_map/pallas_call | solution.py:370
  102.8 0.7 copy.5
Async XLA Ops:
  0.0 0.9 copy-start
  0.9 0.9 copy-start.1
  1.9 0.9 copy-start.2

commit v2 on v0

v2 whole, which is shorter than its diff:
```python
import functools

import jax
import jax.numpy as jnp
from jax import lax
from jax.experimental import pallas as pl
from jax.experimental.pallas import tpu as pltpu
from jax.sharding import PartitionSpec as P

NZ, NY, NX = 8, 8, 4
PAIRS = 3
ROWS, TOK, LANES = 4, 64, 128
EIGHT = TOK // NZ
HALF = NX * EIGHT
F32, BF16 = jnp.float32, jnp.bfloat16


def each(name, *arg):
    return [(name, p) + arg for p in range(PAIRS)]


ORDER = (
    each("q0") + each("k1") + each("q", 0) + each("k", 1) + each("q", 1) + each("k", 2) + each("q", 2) + each("k", 3)
    + each("v1") + each("build") + each("s") + each("z", 1) + each("z", 2) + each("v", 1) + each("z", 3) + each("v", 2)
    + each("local") + each("soft") + each("v", 3) + each("vcat")
)
for k in range(5):
    if k > 0:
        ORDER += each("p", k)
    ORDER += each("o", k) + each("sum", k)
    if k > 0:
        ORDER += each("mid", k - 1)
ORDER += each("mid", 4) + each("fin") + each("out")


def kernel(
    q_hbm, k_hbm, v_hbm, out_hbm,
    kbuf, vbuf, qbuf, qsend, qm, kcat, sbuf, zrecv, stat, statv, pbuf, vcat, obuf, orecv, xhalf, xfull, ofin, oown, oswap,
    load_sem, out_sem, k_ss, k_rs, v_ss, v_rs, qs_ss, qs_rs, qx_ss, qx_rs, qc_ss, qc_rs, z_ss, z_rs, st_ss, st_rs,
    p_ss, p_rs, o_ss, o_rs, xh_ss, xh_rs, xf_ss, xf_rs, w_ss, w_rs,
):
    s_id, r_id = lax.axis_index("seq"), lax.axis_index("res")
    z, yh = s_id // 2, s_id % 2
    yl, x, c = r_id // 8, (r_id // 2) % 4, r_id % 2
    y = yh * 4 + yl

    def at(z_=None, y_=None, x_=None, c_=None):
        z_ = z if z_ is None else z_
        y_ = y if y_ is None else y_
        x_ = x if x_ is None else x_
        c_ = c if c_ is None else c_
        return {"seq": z_ * 2 + y_ // 4, "res": ((y_ % 4) * 4 + x_) * 2 + c_}

    def zdev(k):
        return at(z_=(z + k + NZ) % NZ)

    def ydev(k):
        return at(y_=(y + k + NY) % NY)

    way_out = (yh + c) % 2
    taker = at(y_=(y + 2 - 4 * way_out + NY) % NY, c_=yh)
    way_in = ((y + 6) % NY // 4 + c) % 2
    owner = at(y_=(y - 2 + 4 * way_in + NY) % NY, c_=(c + way_in) % 2)
    sibling = at(c_=1 - c)

    def group(k):
        g = (x * 2 + c + k) % 8
        return at(x_=g // 2, c_=g % 2)

    def group_index(k):
        g = (x * 2 + c + k + 8) % 8
        return g // 2, g % 2

    def remote(src, dst, ss, rs, dev):
        return pltpu.make_async_remote_copy(
            src_ref=src, dst_ref=dst, send_sem=ss, recv_sem=rs, device_id=dev, device_id_type=pl.DeviceIdType.MESH
        )

    sent, due = [], {}

    def go(key, send, recv=None):
        send().start()
        sent.append(send)
        due[key] = recv or send

    def got(key):
        due.pop(key)().wait_recv()

    def lanes(p):
        return pl.ds(p * LANES, LANES)

    def load_k(p):
        return pltpu.make_async_copy(k_hbm.at[:, :, lanes(p)], kbuf.at[p, y], load_sem.at[0, p])

    def load_v(p):
        return pltpu.make_async_copy(v_hbm.at[:, :, lanes(p)], vbuf.at[p, y], load_sem.at[1, p])

    def load_q(p):
        return pltpu.make_async_copy(q_hbm.at[:, :, lanes(p)], qsend.at[p], load_sem.at[2, p])

    def ring(buf, ss, rs, p, step, way):
        src = (y - way * (step - 1) + NY) % NY
        half = pl.ds(0, ROWS) if step < 4 else (pl.ds(0, 2) if way == 1 else pl.ds(2, 2))
        d = 0 if way == 1 else 1
        view = buf.at[p, src, half]
        return remote(view, view, ss.at[p, step - 1, d], rs.at[p, step - 1, d], ydev(way))

    def ring_recv(buf, ss, rs, p, step, way):
        src = (y - way * step + NY) % NY
        half = pl.ds(0, ROWS) if step < 4 else (pl.ds(0, 2) if way == 1 else pl.ds(2, 2))
        d = 0 if way == 1 else 1
        view = buf.at[p, src, half]
        return remote(view, view, ss.at[p, step - 1, d], rs.at[p, step - 1, d], ydev(way))

    K = (kbuf, k_ss, k_rs)
    V = (vbuf, v_ss, v_rs)

    def ring_start(t, p, step):
        for way in (1, -1):
            go((t is K, p, step, way), functools.partial(ring, *t, p, step, way), functools.partial(ring_recv, *t, p, step, way))

    def ring_wait(t, p, step):
        for way in (1, -1):
            got((t is K, p, step, way))

    def q_move(p, slot, dev):
        return remote(qsend.at[p], qbuf.at[p, slot, x], qs_ss.at[p], qs_rs.at[p], dev)

    def q_start(p):
        load_q(p).wait()
        go(("qs", p), lambda: q_move(p, yh, taker), lambda: q_move(p, c, taker))

    def q_ring(p, step, way, behind):
        d = 0 if way == 1 else 1
        half = pl.ds(0, ROWS) if step == 1 else pl.ds(2 * d, 2)
        view = qbuf.at[p, c, (x - way * (step - 1 + behind) + NX) % NX, half]
        return remote(view, view, qx_ss.at[p, step - 1, d], qx_rs.at[p, step - 1, d], at(x_=(x + way + NX) % NX))

    def q_ring_start(p, step):
        for way in (1, -1):
            go(("qx", p, step, way), functools.partial(q_ring, p, step, way, 0), functools.partial(q_ring, p, step, way, 1))

    def q_step(p, step):
        if step == 0:
            got(("qs", p))
        else:
            for way in (1, -1):
                got(("qx", p, step, way))
        if step < 2:
            q_ring_start(p, step + 1)
        else:
            go(("qc", p), functools.partial(q_share, p), functools.partial(q_share_recv, p))

    def q_share(p):
        return remote(qbuf.at[p, c], qbuf.at[p, c], qc_ss.at[p], qc_rs.at[p], sibling)

    def q_share_recv(p):
        return remote(qbuf.at[p, 1 - c], qbuf.at[p, 1 - c], qc_ss.at[p], qc_rs.at[p], sibling)

    def q_spread_start(p, where):
        if where is at_home:
            at_home(lambda: load_q_home(p).wait())
        else:
            got(("qs", p))
        for k in (2, 1, 3):
            go(("qx", p, k, where), functools.partial(q_spread, p, k), functools.partial(q_spread_recv, p, k), where)

    lane = lax.broadcasted_iota(jnp.int32, (HALF, LANES), 1)

    def q_build(p):
        got(("qc", p))
        for g in range(2):
            for r in range(ROWS):
                cols = pl.ds((g * ROWS + r) * LANES, LANES)
                block = qbuf[p, g, :, r].astype(F32)
                for s in range(NZ):
                    part = jnp.concatenate([block[i, s * EIGHT : (s + 1) * EIGHT] for i in range(NX)], axis=0)
                    zero = jnp.zeros_like(part)
                    qm[p, s, 0, :, cols] = jnp.where(lane < 64, part, zero).astype(BF16)
                    qm[p, s, 1, :, cols] = jnp.where(lane >= 64, part, zero).astype(BF16)

    def scores(p):
        ring_wait(K, p, 4)
        for g in range(2):
            for r in range(ROWS):
                cols = pl.ds((g * ROWS + r) * LANES, LANES)
                kcat[:, cols] = kbuf[p, g * 4 : g * 4 + 4, r].reshape(256, LANES)
        for half in range(2):
            part = lax.dot_general(
                qm[p, half * 4 : half * 4 + 4].reshape(256, 1024), kcat[...], (((1,), (1,)), ((), ())), preferred_element_type=F32
            )
            sbuf[p, half * 4 : half * 4 + 4] = part.reshape(4, TOK, 256)
        z_start(p, 1)

    def zslice(way, step):
        return (z + way * (5 - step) + NZ) % NZ

    def z_copy(p, step, way):
        d = 0 if way == 1 else 1
        half = pl.ds(0, TOK) if step > 1 else pl.ds(d * 32, 32)
        return remote(
            sbuf.at[p, zslice(way, step), half],
            zrecv.at[p, d, step - 1, half],
            z_ss.at[p, step - 1, d],
            z_rs.at[p, step - 1, d],
            zdev(way),
        )

    def z_start(p, step):
        for way in (1, -1):
            go(("z", p, step, way), functools.partial(z_copy, p, step, way))

    def z_add(p, step):
        for way in (1, -1):
            d = 0 if way == 1 else 1
            got(("z", p, step, way))
            s = zslice(way, step + 1)
            if step == 1:
                rows = pl.ds(d * 32, 32)
                sbuf[p, s, rows] = sbuf[p, s, rows] + zrecv[p, d, 0, rows]
            else:
                sbuf[p, s] = sbuf[p, s] + zrecv[p, d, step - 1]
        z_start(p, step + 1)

    def stat_copy(p, k):
        return remote(stat.at[p, 0], stat.at[p, k], st_ss.at[p, k - 1], st_rs.at[p, k - 1], group(k))

    def softmax_local(p):
        for way in (1, -1):
            got(("z", p, 4, way))
        s = sbuf[p, z] + zrecv[p, 0, 3] + zrecv[p, 1, 3]
        s = s * (1.0 / 64.0)
        m = jnp.max(s, axis=1, keepdims=True)
        e = jnp.exp(s - m)
        l = jnp.sum(e, axis=1, keepdims=True)
        statv[p] = e
        col = lax.broadcasted_iota(jnp.int32, (TOK, LANES), 1)
        both = jnp.where(col == 0, m, l)
        tall = jnp.concatenate([both, both], axis=0)
        stat[p, 0] = jnp.transpose(tall)[0:8, :]
        for k in range(1, 8):
            go(("st", p, k), functools.partial(stat_copy, p, k))

    def softmax_global(p):
        for k in range(1, 8):
            got(("st", p, k))
        m = stat[p, 0, 0:1, :]
        for k in range(1, 8):
            m = jnp.maximum(m, stat[p, k, 0:1, :])
        l = jnp.zeros_like(m)
        for k in range(8):
            l = l + jnp.exp(stat[p, k, 0:1, :] - m) * stat[p, k, 1:2, :]
        factor = jnp.exp(stat[p, 0, 0:1, :] - m) / l
        tall = jnp.transpose(jnp.broadcast_to(factor, (LANES, LANES)))
        pbuf[p, z] = (statv[p] * tall[0:TOK, 0:1]).astype(BF16)
        p_start(p, 1)

    def p_view(p, step, way, slot):
        half = pl.ds(0, TOK) if step < 4 else pl.ds(0 if way == 1 else 32, 32)
        return pbuf.at[p, (slot + 2 * NZ) % NZ, half]

    def p_copy(p, step, way, behind):
        d = 0 if way == 1 else 1
        view = p_view(p, step, way, z - way * (step - 1 + behind))
        return remote(view, view, p_ss.at[p, step - 1, d], p_rs.at[p, step - 1, d], zdev(way))

    def p_start(p, step):
        for way in (1, -1):
            go(("p", p, step, way), functools.partial(p_copy, p, step, way, 0), functools.partial(p_copy, p, step, way, 1))

    def p_wait(p, step):
        for way in (1, -1):
            got(("p", p, step, way))

    def v_build(p):
        ring_wait(V, p, 4)
        for g in range(2):
            for r in range(ROWS):
                vcat[p, g, :, pl.ds(r * LANES, LANES)] = vbuf[p, g * 4 : g * 4 + 4, r].reshape(256, LANES)

    first = lax.broadcasted_iota(jnp.int32, (HALF, ROWS * LANES), 1) % LANES < 64

    def slices(k):
        if k == 0:
            return [z]
        if k == 4:
            return [(z + 4) % NZ]
        return [(z + NZ - k) % NZ, (z + k) % NZ]

    def line(k):
        return pl.ds(0, 1) if k == 0 else pl.ds(2 * k - 1, 1 if k == 4 else 2)

    def places(k):
        return range(line(k).start, line(k).start + line(k).size)

    def o_copy(p, k):
        return remote(obuf.at[p, 1 - c, line(k)], orecv.at[p, line(k)], o_ss.at[p, k], o_rs.at[p, k], sibling)

    def x_half(p, k, way):
        d = 0 if way == 1 else 1
        return remote(
            obuf.at[p, c, line(k), (x + 2) % NX, :, pl.ds(256 * d, 256)], xhalf.at[p, d, line(k)],
            xh_ss.at[p, k, d], xh_rs.at[p, k, d], at(x_=(x + way + NX) % NX),
        )

    def x_full(p, k, way):
        d = 0 if way == 1 else 1
        to = (x + way + NX) % NX
        return remote(obuf.at[p, c, line(k), to], xfull.at[p, d, line(k)], xf_ss.at[p, k, d], xf_rs.at[p, k, d], at(x_=to))

    def attend(p, k):
        parts = slices(k)
        probs = [pbuf[p, s] for s in parts]
        probs = probs[0] if len(probs) == 1 else jnp.concatenate(probs, axis=0)
        for g in (1 - c, c):
            o = lax.dot_general(probs, vcat[p, g], (((1,), (0,)), ((), ())), preferred_element_type=F32)
            for t in range(len(parts)):
                both = jnp.where(first, o[t * TOK : t * TOK + HALF], o[t * TOK + HALF : (t + 1) * TOK])
                obuf[p, g, line(k).start + t] = both.reshape(NX, EIGHT, ROWS * LANES)
            if g is not c:
                go(("o", p, k), functools.partial(o_copy, p, k))

    def chip_sum(p, k):
        got(("o", p, k))
        for n in places(k):
            obuf[p, c, n] = obuf[p, c, n] + orecv[p, n]
        for way in (1, -1):
            go(("xh", p, k, way), functools.partial(x_half, p, k, way))

    def x_sum(p, k):
        for way in (1, -1):
            d = 0 if way == 1 else 1
            got(("xh", p, k, way))
            to = (x + way + NX) % NX
            cols = pl.ds(256 * d, 256)
            for n in places(k):
                obuf[p, c, n, to, :, cols] = obuf[p, c, n, to, :, cols] + xhalf[p, d, n]
            go(("xf", p, k, way), functools.partial(x_full, p, k, way))

    def out_copy(p):
        return pltpu.make_async_copy(oswap.at[p], out_hbm.at[:, :, lanes(p)], out_sem.at[p])

    def w_copy(p):
        return remote(oown.at[p], oswap.at[p], w_ss.at[p], w_rs.at[p], owner)

    def finish(p):
        for k in range(5):
            for way in (1, -1):
                got(("xf", p, k, way))
            for t, s in enumerate(slices(k)):
                n = line(k).start + t
                ofin[p, s] = obuf[p, c, n, x] + xfull[p, 0, n] + xfull[p, 1, n]
        for r in range(ROWS):
            oown[p, r] = ofin[p, :, :, r * LANES : (r + 1) * LANES].reshape(TOK, LANES).astype(BF16)
        go(("w", p), functools.partial(w_copy, p))

    def leave(p):
        got(("w", p))
        out_copy(p).start()

    pairs = range(PAIRS)
    for p in pairs:
        load_q(p).start()
        load_k(p).start()
    for p in pairs:
        load_v(p).start()

    barrier = pltpu.get_barrier_semaphore()
    peers = [zdev(1), zdev(-1), ydev(1), ydev(-1), taker, owner] + [group(k) for k in range(1, 8)]
    for dev in peers:
        pl.semaphore_signal(barrier, inc=1, device_id=dev, device_id_type=pl.DeviceIdType.MESH)
    pl.semaphore_wait(barrier, len(peers))

    def schedule():
        def k_step(p, step):
            ring_wait(K, p, step)
            ring_start(K, p, step + 1)

        def v_step(p, step):
            ring_wait(V, p, step)
            ring_start(V, p, step + 1)

        def k_first(p):
            load_k(p).wait()
            ring_start(K, p, 1)

        def v_first(p):
            load_v(p).wait()
            ring_start(V, p, 1)

        def p_step(p, k):
            p_wait(p, k)
            if k < 4:
                p_start(p, k + 1)

        act = dict(
            q0=q_start, q=q_step, build=q_build, k1=k_first, k=k_step, s=scores, z=z_add, local=softmax_local,
            soft=softmax_global, v1=v_first, v=v_step, vcat=v_build, p=p_step, o=attend, sum=chip_sum, mid=x_sum,
            fin=finish, out=leave,
        )
        for name, *arg in ORDER:
            act[name](*arg)

    schedule()

    for copy in due.values():
        copy().wait_recv()
    for copy in sent:
        copy().wait_send()
    for p in pairs:
        out_copy(p).wait()


def local(queries, keys, values):
    vmem = pltpu.VMEM
    dma = pltpu.SemaphoreType.DMA
    block = (ROWS, TOK, LANES)
    return pl.pallas_call(
        kernel,
        out_shape=jax.ShapeDtypeStruct(queries.shape, BF16),
        in_specs=[pl.BlockSpec(memory_space=pl.ANY)] * 3,
        out_specs=pl.BlockSpec(memory_space=pl.ANY),
        scratch_shapes=[
            vmem((PAIRS, NY) + block, BF16),
            vmem((PAIRS, NY) + block, BF16),
            vmem((PAIRS, 2, NX) + block, BF16),
            vmem((PAIRS,) + block, BF16),
            vmem((PAIRS, NZ, 2, HALF, 1024), BF16),
            vmem((256, 1024), BF16),
            vmem((PAIRS, NZ, TOK, 256), F32),
            vmem((PAIRS, 2, 4, TOK, 256), F32),
            vmem((PAIRS, 8, 8, LANES), F32),
            vmem((PAIRS, TOK, 256), F32),
            vmem((PAIRS, NZ, TOK, 256), BF16),
            vmem((PAIRS, 2, 256, 512), BF16),
            vmem((PAIRS, 2, NZ, NX, EIGHT, 512), F32),
            vmem((PAIRS, NZ, NX, EIGHT, 512), F32),
            vmem((PAIRS, 2, NZ, EIGHT, 256), F32),
            vmem((PAIRS, 2, NZ, EIGHT, 512), F32),
            vmem((PAIRS, NZ, EIGHT, 512), F32),
            vmem((PAIRS,) + block, BF16),
            vmem((PAIRS,) + block, BF16),
            dma((3, PAIRS)),
            dma((PAIRS,)),
            dma((PAIRS, 4, 2)), dma((PAIRS, 4, 2)),
            dma((PAIRS, 4, 2)), dma((PAIRS, 4, 2)),
            dma((PAIRS,)), dma((PAIRS,)),
            dma((PAIRS, 2, 2)), dma((PAIRS, 2, 2)),
            dma((PAIRS,)), dma((PAIRS,)),
            dma((PAIRS, 4, 2)), dma((PAIRS, 4, 2)),
            dma((PAIRS, 7)), dma((PAIRS, 7)),
            dma((PAIRS, 4, 2)), dma((PAIRS, 4, 2)),
            dma((PAIRS, 5)), dma((PAIRS, 5)),
            dma((PAIRS, 5, 2)), dma((PAIRS, 5, 2)),
            dma((PAIRS, 5, 2)), dma((PAIRS, 5, 2)),
            dma((PAIRS,)), dma((PAIRS,)),
        ],
        compiler_params=pltpu.CompilerParams(collective_id=0, has_side_effects=True, vmem_limit_bytes=63 << 20),
    )(queries, keys, values)


def solution(mesh):
    spec = P("seq", "res", None)
    return jax.shard_map(local, mesh=mesh, in_specs=(spec, spec, spec), out_specs=spec, check_vma=False)
```

time: 481 us -> 96.7 us (0.20)
  waiting for transfers between devices: 423 us -> 0 us
  Pallas kernels: 0 us -> 94.8 us
  local copies, waits for them, and re-layouts: 27.3 us -> 1.62 us
  between operations: 13.1 us -> 0.01 us
  matrix products: 12.7 us -> 0 us
    psum x1 -> x0, waiting for transfers between devices: 296 us -> none  [local(): summed = lax.psum(partial_value, 'seq') * scale]
    all_gather x2 -> x0, waiting for transfers between devices: 127 us -> none  [the longest x1 72.8 us: local(): piece = lax.all_gather(keys, 'res', axis=1, tiled=True)]
    pallas_call x0 -> x1, Pallas kernels: none -> 94.8 us  [local(): pl.pallas_call(kernel, out_shape=jax.ShapeDtypeStruct(queries.shape, BF16...]
    all_gather x2 -> x0, local copies, waits for them, and re-layouts: 21.2 us -> none  [the longest x1 10.6 us: local(): piece = lax.all_gather(values, 'res', axis=1, tiled=True)]
    dot_general x2 -> x0, matrix products: 12.7 us -> none  [the longest x1 6.95 us: local(): jnp.einsum('hij,rjhe->rihe', probs, value_four, preferred_element_type=jn...]
  transfers between devices with their start and end apart: 3 -> 0, of which waited for: 3 -> 0; matrix products, arithmetic and copies ran while one was open for 6% -> 0% of each run, Pallas kernels for 0% -> 0%
where the time goes in v2:
time: 96.7 us; the launch traced here: 96.4 us
  Pallas kernels  94.8 us (98%)
  local copies, waits for them, and re-layouts  1.62 us (2%)
    pallas_call x1, Pallas kernels, local(): pl.pallas_call(kernel, out_shape=jax.ShapeDtypeStruct(queries.shape, BF16...  94.8 us

profile of v2, /device:TPU:1, one launch (start us, length us, event | category | flops | bytes accessed | tf_op | source)
XLA Modules:
  0.0 96.4 jit_solution(3090661807512024463)
XLA Ops:
  0.0 94.8 %shard_map.37 = bf16[4,64,384]{2,1,0:T(8,128)(2,1)} custom-call(bf16[4,64,384]{2,1,0:T(8,128)(2,1)} %q_hbm.1, bf16[4,64,384]{2,1,0:T(8,128)(2,1)} %k_hbm.1, bf16[4,64,384]{2,1,0:T(8,128)(2,1)} %v_hbm.1), custom_call_target="tpu_custom_call" | custom-call | tf_op jit(solution)/shard_map/pallas_call | solution.py:418
  94.8 1.6 %copy.5 = bf16[4,64,384]{2,1,0:T(8,128)(2,1)} copy(bf16[4,64,384]{2,1,0:T(8,128)(2,1)} %shard_map.37) | data formatting | bytes 393216

commit v3 on v2

--- a/solution.py
+++ b/solution.py
@@ -15,28 +15,29 @@
 F32, BF16 = jnp.float32, jnp.bfloat16
 
 
-def each(name, *arg):
-    return [(name, p) + arg for p in range(PAIRS)]
-
-
-ORDER = (
-    each("q0") + each("k1") + each("q", 0) + each("k", 1) + each("q", 1) + each("k", 2) + each("q", 2) + each("k", 3)
-    + each("v1") + each("build") + each("s") + each("z", 1) + each("z", 2) + each("v", 1) + each("z", 3) + each("v", 2)
-    + each("local") + each("soft") + each("v", 3) + each("vcat")
-)
-for k in range(5):
-    if k > 0:
-        ORDER += each("p", k)
-    ORDER += each("o", k) + each("sum", k)
-    if k > 0:
-        ORDER += each("mid", k - 1)
-ORDER += each("mid", 4) + each("fin") + each("out")
+ORDER = [
+    ("q0", 0), ("q0", 1), ("q0", 2), ("qw", 0), ("qw", 1), ("qw", 2), ("k1", 0), ("k1", 1), ("k1", 2), ("q", 0, 0),
+    ("q", 1, 0), ("q", 2, 0), ("k", 0, 1), ("k", 1, 1), ("k", 2, 1), ("q", 0, 1), ("q", 1, 1), ("q", 2, 1),
+    ("k", 0, 2), ("k", 1, 2), ("k", 2, 2), ("q", 0, 2), ("q", 1, 2), ("q", 2, 2), ("k", 0, 3), ("k", 1, 3),
+    ("k", 2, 3), ("v1", 0), ("v1", 1), ("v1", 2), ("build", 0), ("build", 1), ("build", 2), ("s", 0), ("s", 1),
+    ("s", 2), ("z", 0, 1), ("z", 1, 1), ("z", 2, 1), ("v", 0, 1), ("v", 1, 1), ("v", 2, 1), ("z", 0, 2), ("z", 1, 2),
+    ("z", 2, 2), ("v", 0, 2), ("v", 1, 2), ("v", 2, 2), ("z", 0, 3), ("z", 1, 3), ("z", 2, 3), ("v", 0, 3),
+    ("v", 1, 3), ("v", 2, 3), ("local", 0), ("local", 1), ("local", 2), ("soft", 0), ("soft", 1), ("soft", 2),
+    ("vcat", 0), ("vcat", 1), ("vcat", 2), ("o", 0, 0), ("o", 1, 0), ("o", 2, 0), ("sum", 0, 0), ("sum", 1, 0),
+    ("sum", 2, 0), ("p", 0, 1), ("p", 1, 1), ("p", 2, 1), ("o", 0, 1), ("o", 1, 1), ("o", 2, 1), ("sum", 0, 1),
+    ("sum", 1, 1), ("sum", 2, 1), ("mid", 0, 0), ("mid", 1, 0), ("mid", 2, 0), ("p", 0, 2), ("p", 1, 2), ("p", 2, 2),
+    ("o", 0, 2), ("o", 1, 2), ("o", 2, 2), ("sum", 0, 2), ("sum", 1, 2), ("sum", 2, 2), ("mid", 0, 1), ("mid", 1, 1),
+    ("mid", 2, 1), ("p", 0, 3), ("p", 1, 3), ("p", 2, 3), ("o", 0, 3), ("o", 1, 3), ("o", 2, 3), ("sum", 0, 3),
+    ("sum", 1, 3), ("sum", 2, 3), ("mid", 0, 2), ("mid", 1, 2), ("mid", 2, 2), ("p", 0, 4), ("o", 0, 4),
+    ("sum", 0, 4), ("p", 1, 4), ("o", 1, 4), ("sum", 1, 4), ("p", 2, 4), ("o", 2, 4), ("sum", 2, 4), ("mid", 0, 3),
+    ("mid", 1, 3), ("mid", 2, 3), ("fin", 0), ("fin", 1), ("fin", 2),
+]
 
 
 def kernel(
     q_hbm, k_hbm, v_hbm, out_hbm,
-    kbuf, vbuf, qbuf, qsend, qm, kcat, sbuf, zrecv, stat, statv, pbuf, vcat, obuf, orecv, xhalf, xfull, ofin, oown, oswap,
-    load_sem, out_sem, k_ss, k_rs, v_ss, v_rs, qs_ss, qs_rs, qx_ss, qx_rs, qc_ss, qc_rs, z_ss, z_rs, st_ss, st_rs,
+    kbuf, vbuf, qbuf, qsend, qm, kcat, sbuf, zrecv, stat, statv, pbuf, vcat, obuf, orecv, xhalf, xfull, ofin, oown,
+    load_sem, k_ss, k_rs, v_ss, v_rs, qs_ss, qs_rs, qx_ss, qx_rs, qc_ss, qc_rs, z_ss, z_rs, st_ss, st_rs,
     p_ss, p_rs, o_ss, o_rs, xh_ss, xh_rs, xf_ss, xf_rs, w_ss, w_rs,
 ):
     s_id, r_id = lax.axis_index("seq"), lax.axis_index("res")
@@ -76,15 +77,19 @@
             src_ref=src, dst_ref=dst, send_sem=ss, recv_sem=rs, device_id=dev, device_id_type=pl.DeviceIdType.MESH
         )
 
-    sent, due = [], {}
+    sent, due = {}, {}
 
     def go(key, send, recv=None):
         send().start()
-        sent.append(send)
+        sent[key] = send
         due[key] = recv or send
 
     def got(key):
         due.pop(key)().wait_recv()
+
+    def left(*keys):
+        for key in keys:
+            sent.pop(key)().wait_send()
 
     def lanes(p):
         return pl.ds(p * LANES, LANES)
@@ -304,7 +309,7 @@
         )
 
     def x_full(p, k, way):
-        d = 0 if way == 1 else 1
+        d = (1, -1, 2).index(way)
         to = (x + way + NX) % NX
         return remote(obuf.at[p, c, line(k), to], xfull.at[p, d, line(k)], xf_ss.at[p, k, d], xf_rs.at[p, k, d], at(x_=to))
 
@@ -324,6 +329,10 @@
         got(("o", p, k))
         for n in places(k):
             obuf[p, c, n] = obuf[p, c, n] + orecv[p, n]
+        if k == 4:
+            for way in (2, 1, -1):
+                go(("xf", p, k, way), functools.partial(x_full, p, k, way))
+            return
         for way in (1, -1):
             go(("xh", p, k, way), functools.partial(x_half, p, k, way))
 
@@ -337,26 +346,20 @@
                 obuf[p, c, n, to, :, cols] = obuf[p, c, n, to, :, cols] + xhalf[p, d, n]
             go(("xf", p, k, way), functools.partial(x_full, p, k, way))
 
-    def out_copy(p):
-        return pltpu.make_async_copy(oswap.at[p], out_hbm.at[:, :, lanes(p)], out_sem.at[p])
-
     def w_copy(p):
-        return remote(oown.at[p], oswap.at[p], w_ss.at[p], w_rs.at[p], owner)
+        return remote(oown.at[p], out_hbm.at[:, :, lanes(p)], w_ss.at[p], w_rs.at[p], owner)
 
     def finish(p):
         for k in range(5):
-            for way in (1, -1):
+            for way in (1, -1) if k < 4 else (1, -1, 2):
                 got(("xf", p, k, way))
             for t, s in enumerate(slices(k)):
                 n = line(k).start + t
-                ofin[p, s] = obuf[p, c, n, x] + xfull[p, 0, n] + xfull[p, 1, n]
+                total = obuf[p, c, n, x] + xfull[p, 0, n] + xfull[p, 1, n]
+                ofin[p, s] = total if k < 4 else total + xfull[p, 2, n]
         for r in range(ROWS):
             oown[p, r] = ofin[p, :, :, r * LANES : (r + 1) * LANES].reshape(TOK, LANES).astype(BF16)
         go(("w", p), functools.partial(w_copy, p))
-
-    def leave(p):
-        got(("w", p))
-        out_copy(p).start()
 
     pairs = range(PAIRS)
     for p in pairs:
@@ -396,7 +399,8 @@
         act = dict(
             q0=q_start, q=q_step, build=q_build, k1=k_first, k=k_step, s=scores, z=z_add, local=softmax_local,
             soft=softmax_global, v1=v_first, v=v_step, vcat=v_build, p=p_step, o=attend, sum=chip_sum, mid=x_sum,
-            fin=finish, out=leave,
+            fin=finish, qw=lambda p: left(("qs", p)), kw=lambda p: left((True, p, 1, 1), (True, p, 1, -1)),
+            pw=lambda p: left(("p", p, 1, 1), ("p", p, 1, -1)),
         )
         for name, *arg in ORDER:
             act[name](*arg)
@@ -405,10 +409,8 @@
 
     for copy in due.values():
         copy().wait_recv()
-    for copy in sent:
+    for copy in sent.values():
         copy().wait_send()
-    for p in pairs:
-        out_copy(p).wait()
 
 
 def local(queries, keys, values):
@@ -436,12 +438,10 @@
             vmem((PAIRS, 2, NZ, NX, EIGHT, 512), F32),
             vmem((PAIRS, NZ, NX, EIGHT, 512), F32),
             vmem((PAIRS, 2, NZ, EIGHT, 256), F32),
-            vmem((PAIRS, 2, NZ, EIGHT, 512), F32),
+            vmem((PAIRS, 3, NZ, EIGHT, 512), F32),
             vmem((PAIRS, NZ, EIGHT, 512), F32),
             vmem((PAIRS,) + block, BF16),
-            vmem((PAIRS,) + block, BF16),
             dma((3, PAIRS)),
-            dma((PAIRS,)),
             dma((PAIRS, 4, 2)), dma((PAIRS, 4, 2)),
             dma((PAIRS, 4, 2)), dma((PAIRS, 4, 2)),
             dma((PAIRS,)), dma((PAIRS,)),
@@ -452,7 +452,7 @@
             dma((PAIRS, 4, 2)), dma((PAIRS, 4, 2)),
             dma((PAIRS, 5)), dma((PAIRS, 5)),
             dma((PAIRS, 5, 2)), dma((PAIRS, 5, 2)),
-            dma((PAIRS, 5, 2)), dma((PAIRS, 5, 2)),
+            dma((PAIRS, 5, 3)), dma((PAIRS, 5, 3)),
             dma((PAIRS,)), dma((PAIRS,)),
         ],
         compiler_params=pltpu.CompilerParams(collective_id=0, has_side_effects=True, vmem_limit_bytes=63 << 20),

time: 96.7 us -> 93 us (0.962)
  Pallas kernels: 94.8 us -> 91 us
    pallas_call x1, Pallas kernels: 94.8 us -> 91 us  [local(): pl.pallas_call(kernel, out_shape=jax.ShapeDtypeStruct(queries.shape, BF16...]
where the time goes in v3:
time: 93 us; the launch traced here: 92.7 us
  Pallas kernels  91 us (98%)
  local copies, waits for them, and re-layouts  1.62 us (2%)
    pallas_call x1, Pallas kernels, local(): pl.pallas_call(kernel, out_shape=jax.ShapeDtypeStruct(queries.shape, BF16...  91 us

profile of v3, /device:TPU:1, one launch (start us, length us, event | category | flops | bytes accessed | tf_op | source)
XLA Modules:
  0.0 92.7 jit_solution(3995673152353659640)
XLA Ops:
  0.0 91.0 %shard_map.37 = bf16[4,64,384]{2,1,0:T(8,128)(2,1)} custom-call(bf16[4,64,384]{2,1,0:T(8,128)(2,1)} %q_hbm.1, bf16[4,64,384]{2,1,0:T(8,128)(2,1)} %k_hbm.1, bf16[4,64,384]{2,1,0:T(8,128)(2,1)} %v_hbm.1), custom_call_target="tpu_custom_call" | custom-call | tf_op jit(solution)/shard_map/pallas_call | solution.py:420
  91.0 1.6 %copy.5 = bf16[4,64,384]{2,1,0:T(8,128)(2,1)} copy(bf16[4,64,384]{2,1,0:T(8,128)(2,1)} %shard_map.37) | data formatting | bytes 393216

commit v4 on v3

--- a/solution.py
+++ b/solution.py
@@ -16,21 +16,22 @@
 
 
 ORDER = [
-    ("q0", 0), ("q0", 1), ("q0", 2), ("qw", 0), ("qw", 1), ("qw", 2), ("k1", 0), ("k1", 1), ("k1", 2), ("q", 0, 0),
-    ("q", 1, 0), ("q", 2, 0), ("k", 0, 1), ("k", 1, 1), ("k", 2, 1), ("q", 0, 1), ("q", 1, 1), ("q", 2, 1),
-    ("k", 0, 2), ("k", 1, 2), ("k", 2, 2), ("q", 0, 2), ("q", 1, 2), ("q", 2, 2), ("k", 0, 3), ("k", 1, 3),
-    ("k", 2, 3), ("v1", 0), ("v1", 1), ("v1", 2), ("build", 0), ("build", 1), ("build", 2), ("s", 0), ("s", 1),
-    ("s", 2), ("z", 0, 1), ("z", 1, 1), ("z", 2, 1), ("v", 0, 1), ("v", 1, 1), ("v", 2, 1), ("z", 0, 2), ("z", 1, 2),
-    ("z", 2, 2), ("v", 0, 2), ("v", 1, 2), ("v", 2, 2), ("z", 0, 3), ("z", 1, 3), ("z", 2, 3), ("v", 0, 3),
-    ("v", 1, 3), ("v", 2, 3), ("local", 0), ("local", 1), ("local", 2), ("soft", 0), ("soft", 1), ("soft", 2),
-    ("vcat", 0), ("vcat", 1), ("vcat", 2), ("o", 0, 0), ("o", 1, 0), ("o", 2, 0), ("sum", 0, 0), ("sum", 1, 0),
-    ("sum", 2, 0), ("p", 0, 1), ("p", 1, 1), ("p", 2, 1), ("o", 0, 1), ("o", 1, 1), ("o", 2, 1), ("sum", 0, 1),
-    ("sum", 1, 1), ("sum", 2, 1), ("mid", 0, 0), ("mid", 1, 0), ("mid", 2, 0), ("p", 0, 2), ("p", 1, 2), ("p", 2, 2),
-    ("o", 0, 2), ("o", 1, 2), ("o", 2, 2), ("sum", 0, 2), ("sum", 1, 2), ("sum", 2, 2), ("mid", 0, 1), ("mid", 1, 1),
-    ("mid", 2, 1), ("p", 0, 3), ("p", 1, 3), ("p", 2, 3), ("o", 0, 3), ("o", 1, 3), ("o", 2, 3), ("sum", 0, 3),
-    ("sum", 1, 3), ("sum", 2, 3), ("mid", 0, 2), ("mid", 1, 2), ("mid", 2, 2), ("p", 0, 4), ("o", 0, 4),
-    ("sum", 0, 4), ("p", 1, 4), ("o", 1, 4), ("sum", 1, 4), ("p", 2, 4), ("o", 2, 4), ("sum", 2, 4), ("mid", 0, 3),
-    ("mid", 1, 3), ("mid", 2, 3), ("fin", 0), ("fin", 1), ("fin", 2),
+    ("q0", 0), ("q0", 1), ("q0", 2), ("qw", 0), ("qw", 1), ("qw", 2), ("k1", 0), ("k1", 1), ("k1", 2), ("vl", 0),
+    ("vl", 1), ("vl", 2), ("q", 0, 0), ("q", 1, 0), ("q", 2, 0), ("k", 0, 1), ("k", 1, 1), ("k", 2, 1), ("q", 0, 1),
+    ("q", 1, 1), ("q", 2, 1), ("k", 0, 2), ("k", 1, 2), ("k", 2, 2), ("q", 0, 2), ("q", 1, 2), ("q", 2, 2),
+    ("k", 0, 3), ("k", 1, 3), ("k", 2, 3), ("v1", 0), ("v1", 1), ("v1", 2), ("build", 0), ("build", 1), ("build", 2),
+    ("s", 0), ("s", 1), ("s", 2), ("z", 0, 1), ("z", 1, 1), ("z", 2, 1), ("v", 0, 1), ("v", 1, 1), ("v", 2, 1),
+    ("z", 0, 2), ("z", 1, 2), ("z", 2, 2), ("v", 0, 2), ("v", 1, 2), ("v", 2, 2), ("z", 0, 3), ("z", 1, 3),
+    ("z", 2, 3), ("v", 0, 3), ("v", 1, 3), ("v", 2, 3), ("local", 0), ("local", 1), ("local", 2), ("soft", 0),
+    ("soft", 1), ("soft", 2), ("vcat", 0), ("vcat", 1), ("vcat", 2), ("o", 0, 0), ("o", 1, 0), ("o", 2, 0),
+    ("sum", 0, 0), ("sum", 1, 0), ("sum", 2, 0), ("p", 0, 1), ("p", 1, 1), ("p", 2, 1), ("o", 0, 1), ("o", 1, 1),
+    ("o", 2, 1), ("sum", 0, 1), ("sum", 1, 1), ("sum", 2, 1), ("mid", 0, 0), ("mid", 1, 0), ("mid", 2, 0),
+    ("p", 0, 2), ("p", 1, 2), ("p", 2, 2), ("o", 0, 2), ("o", 1, 2), ("o", 2, 2), ("sum", 0, 2), ("sum", 1, 2),
+    ("sum", 2, 2), ("mid", 0, 1), ("mid", 1, 1), ("mid", 2, 1), ("p", 0, 3), ("p", 1, 3), ("p", 2, 3), ("o", 0, 3),
+    ("o", 1, 3), ("o", 2, 3), ("sum", 0, 3), ("sum", 1, 3), ("sum", 2, 3), ("mid", 0, 2), ("mid", 1, 2),
+    ("mid", 2, 2), ("mid", 0, 3), ("mid", 1, 3), ("mid", 2, 3), ("p", 0, 4), ("o", 0, 4), ("sum", 0, 4), ("p", 1, 4),
+    ("o", 1, 4), ("sum", 1, 4), ("p", 2, 4), ("o", 2, 4), ("sum", 2, 4), ("most", 0), ("most", 1), ("most", 2),
+    ("fin", 0), ("fin", 1), ("fin", 2),
 ]
 
 
@@ -346,28 +347,40 @@
                 obuf[p, c, n, to, :, cols] = obuf[p, c, n, to, :, cols] + xhalf[p, d, n]
             go(("xf", p, k, way), functools.partial(x_full, p, k, way))
 
-    def w_copy(p):
-        return remote(oown.at[p], out_hbm.at[:, :, lanes(p)], w_ss.at[p], w_rs.at[p], owner)
+    def w_copy(p, i):
+        rows = pl.ds(pl.multiple_of(((z + 4) % NZ // 2 + i) % NX * 16, 16), 16)
+        return remote(oown.at[p, :, rows], out_hbm.at[:, rows, lanes(p)], w_ss.at[p, i], w_rs.at[p, i], owner)
+
+    def totals(p, k):
+        for way in (1, -1) if k < 4 else (1, -1, 2):
+            got(("xf", p, k, way))
+        for t, s in enumerate(slices(k)):
+            n = line(k).start + t
+            total = obuf[p, c, n, x] + xfull[p, 0, n] + xfull[p, 1, n]
+            ofin[p, s] = total if k < 4 else total + xfull[p, 2, n]
+
+    def w_start(p, i):
+        g = ((z + 4) % NZ // 2 + i) % NX
+        rows = pl.ds(pl.multiple_of(g * 16, 16), 16)
+        both = ofin[p, pl.ds(g * 2, 2)].reshape(16, ROWS * LANES)
+        for r in range(ROWS):
+            oown[p, r, rows, :] = both[:, r * LANES : (r + 1) * LANES].astype(BF16)
+        go(("w", p, i), functools.partial(w_copy, p, i))
+
+    def finish_most(p):
+        for k in range(4):
+            totals(p, k)
+        for i in (1, 2, 3):
+            w_start(p, i)
 
     def finish(p):
-        for k in range(5):
-            for way in (1, -1) if k < 4 else (1, -1, 2):
-                got(("xf", p, k, way))
-            for t, s in enumerate(slices(k)):
-                n = line(k).start + t
-                total = obuf[p, c, n, x] + xfull[p, 0, n] + xfull[p, 1, n]
-                ofin[p, s] = total if k < 4 else total + xfull[p, 2, n]
-        for r in range(ROWS):
-            oown[p, r] = ofin[p, :, :, r * LANES : (r + 1) * LANES].reshape(TOK, LANES).astype(BF16)
-        go(("w", p), functools.partial(w_copy, p))
+        totals(p, 4)
+        w_start(p, 0)
 
     pairs = range(PAIRS)
     for p in pairs:
         load_q(p).start()
         load_k(p).start()
-    for p in pairs:
-        load_v(p).start()
-
     barrier = pltpu.get_barrier_semaphore()
     peers = [zdev(1), zdev(-1), ydev(1), ydev(-1), taker, owner] + [group(k) for k in range(1, 8)]
     for dev in peers:
@@ -399,7 +412,7 @@
         act = dict(
             q0=q_start, q=q_step, build=q_build, k1=k_first, k=k_step, s=scores, z=z_add, local=softmax_local,
             soft=softmax_global, v1=v_first, v=v_step, vcat=v_build, p=p_step, o=attend, sum=chip_sum, mid=x_sum,
-            fin=finish, qw=lambda p: left(("qs", p)), kw=lambda p: left((True, p, 1, 1), (True, p, 1, -1)),
+            vl=lambda p: load_v(p).start(), most=finish_most, fin=finish, qw=lambda p: left(("qs", p)), kw=lambda p: left((True, p, 1, 1), (True, p, 1, -1)),
             pw=lambda p: left(("p", p, 1, 1), ("p", p, 1, -1)),
         )
         for name, *arg in ORDER:
@@ -453,7 +466,7 @@
             dma((PAIRS, 5)), dma((PAIRS, 5)),
             dma((PAIRS, 5, 2)), dma((PAIRS, 5, 2)),
             dma((PAIRS, 5, 3)), dma((PAIRS, 5, 3)),
-            dma((PAIRS,)), dma((PAIRS,)),
+            dma((PAIRS, 4)), dma((PAIRS, 4)),
         ],
         compiler_params=pltpu.CompilerParams(collective_id=0, has_side_effects=True, vmem_limit_bytes=63 << 20),
     )(queries, keys, values)

time: 93 us -> 92.4 us (level)
  no operation moved by 1% of the time
where the time goes in v4:
time: 92.4 us; the launch traced here: 92.2 us
  Pallas kernels  90.6 us (98%)
  local copies, waits for them, and re-layouts  1.62 us (2%)
    pallas_call x1, Pallas kernels, local(): pl.pallas_call(kernel, out_shape=jax.ShapeDtypeStruct(queries.shape, BF16...  90.6 us

profile of v4, /device:TPU:1, one launch (start us, length us, event | category | flops | bytes accessed | tf_op | source)
XLA Modules:
  0.0 92.2 jit_solution(12430502492590190569)
XLA Ops:
  0.0 90.6 %shard_map.37 = bf16[4,64,384]{2,1,0:T(8,128)(2,1)} custom-call(bf16[4,64,384]{2,1,0:T(8,128)(2,1)} %q_hbm.1, bf16[4,64,384]{2,1,0:T(8,128)(2,1)} %k_hbm.1, bf16[4,64,384]{2,1,0:T(8,128)(2,1)} %v_hbm.1), custom_call_target="tpu_custom_call" | custom-call | tf_op jit(solution)/shard_map/pallas_call | solution.py:433
  90.6 1.6 %copy.5 = bf16[4,64,384]{2,1,0:T(8,128)(2,1)} copy(bf16[4,64,384]{2,1,0:T(8,128)(2,1)} %shard_map.37) | data formatting | bytes 393216

commit v5 on v4

--- a/solution.py
+++ b/solution.py
@@ -29,7 +29,7 @@
     ("p", 0, 2), ("p", 1, 2), ("p", 2, 2), ("o", 0, 2), ("o", 1, 2), ("o", 2, 2), ("sum", 0, 2), ("sum", 1, 2),
     ("sum", 2, 2), ("mid", 0, 1), ("mid", 1, 1), ("mid", 2, 1), ("p", 0, 3), ("p", 1, 3), ("p", 2, 3), ("o", 0, 3),
     ("o", 1, 3), ("o", 2, 3), ("sum", 0, 3), ("sum", 1, 3), ("sum", 2, 3), ("mid", 0, 2), ("mid", 1, 2),
-    ("mid", 2, 2), ("mid", 0, 3), ("mid", 1, 3), ("mid", 2, 3), ("p", 0, 4), ("o", 0, 4), ("sum", 0, 4), ("p", 1, 4),
+    ("mid", 2, 2), ("p", 0, 4), ("o", 0, 4), ("sum", 0, 4), ("p", 1, 4),
     ("o", 1, 4), ("sum", 1, 4), ("p", 2, 4), ("o", 2, 4), ("sum", 2, 4), ("most", 0), ("most", 1), ("most", 2),
     ("fin", 0), ("fin", 1), ("fin", 2),
 ]
@@ -330,7 +330,7 @@
         got(("o", p, k))
         for n in places(k):
             obuf[p, c, n] = obuf[p, c, n] + orecv[p, n]
-        if k == 4:
+        if k > 2:
             for way in (2, 1, -1):
                 go(("xf", p, k, way), functools.partial(x_full, p, k, way))
             return
@@ -352,12 +352,12 @@
         return remote(oown.at[p, :, rows], out_hbm.at[:, rows, lanes(p)], w_ss.at[p, i], w_rs.at[p, i], owner)
 
     def totals(p, k):
-        for way in (1, -1) if k < 4 else (1, -1, 2):
+        for way in (1, -1) if k < 3 else (1, -1, 2):
             got(("xf", p, k, way))
         for t, s in enumerate(slices(k)):
             n = line(k).start + t
             total = obuf[p, c, n, x] + xfull[p, 0, n] + xfull[p, 1, n]
-            ofin[p, s] = total if k < 4 else total + xfull[p, 2, n]
+            ofin[p, s] = total if k < 3 else total + xfull[p, 2, n]
 
     def w_start(p, i):
         g = ((z + 4) % NZ // 2 + i) % NX

time: 92.4 us -> 92.4 us (level)
  no operation moved by 1% of the time
where the time goes in v5:
time: 92.4 us; the launch traced here: 92.3 us
  Pallas kernels  90.6 us (98%)
  local copies, waits for them, and re-layouts  1.62 us (2%)
    pallas_call x1, Pallas kernels, local(): pl.pallas_call(kernel, out_shape=jax.ShapeDtypeStruct(queries.shape, BF16...  90.6 us

profile of v5, /device:TPU:1, one launch (start us, length us, event | category | flops | bytes accessed | tf_op | source)
XLA Modules:
  0.0 92.3 jit_solution(1630313448437563897)
XLA Ops:
  0.0 90.6 %shard_map.37 = bf16[4,64,384]{2,1,0:T(8,128)(2,1)} custom-call(bf16[4,64,384]{2,1,0:T(8,128)(2,1)} %q_hbm.1, bf16[4,64,384]{2,1,0:T(8,128)(2,1)} %k_hbm.1, bf16[4,64,384]{2,1,0:T(8,128)(2,1)} %v_hbm.1), custom_call_target="tpu_custom_call" | custom-call | tf_op jit(solution)/shard_map/pallas_call | solution.py:433
  90.6 1.6 %copy.5 = bf16[4,64,384]{2,1,0:T(8,128)(2,1)} copy(bf16[4,64,384]{2,1,0:T(8,128)(2,1)} %shard_map.37) | data formatting | bytes 393216
